TPU v7x, 32 devices: a whole 2x2x4 slice. The times are simulated.
32 devices in a mesh: left: 4 (over x, core), right: 8 (over z, y).
Axes of the slice: x: 2, y: 2, z: 4, core: 2. Of those that a mesh axis runs over, the one named last changes fastest.
Arguments:
- left_table: bfloat16 [8192, 256], P('left'), may hold values from -1.5 to 1.5
- right_table: bfloat16 [4, 4096, 256], P('left', 'right'), may hold values from -1.5 to 1.5
- relations: float32 [512, 256], replicated, may hold values from -6 to 6
- source_ids: int32 [4, 8, 1024], P('left', 'right'), may hold values from 0 to 2047
- relation_ids: int32 [4, 8, 1024], P('left', 'right'), may hold values from 0 to 511
- target_ids: int32 [4, 8, 1024], P('left', 'right'), may hold values from 0 to 511
- negative_ids: int32 [4, 8, 1, 1024], P('left', 'right'), may hold values from 0 to 511
- edge_counts: int32 [4, 8], P('left', 'right'), may hold values from 1 to 1024
Outputs:
- left_next: bfloat16 [8192, 256], P('left')
- right_next: bfloat16 [4, 4096, 256], P('left', 'right')
- relations_next: float32 [512, 256], replicated
Inputs may be any that keep to these rules, and one draw needn't show every extreme that they name: Edge slots at positions from edge_counts to 1023 hold ids but are padding.
All inputs are finite; a program needn't handle non-finite values.
Results may differ from a plain program's by a relative error of at most 0.0013.
Values may be sent and summed in bfloat16 or wider, within the bound.
A program may use at most 64 MiB of HBM per device.

v0:
```python
import jax
import jax.numpy as jnp
from jax import lax
from jax.sharding import PartitionSpec as P

step_size = 0.5
relation_step = 12.0


def passed_along(array, axis, by):
    peers = lax.axis_size(axis)
    return lax.ppermute(array, axis, [(i, (i + by) % peers) for i in range(peers)])


def block_terms(left_blk, right_blk, relations, src, kind, dst, neg, live):
    half = relations.shape[1] // 2
    head = jnp.take(left_blk, src, axis=0).astype(jnp.float32)
    tail = jnp.take(right_blk, dst, axis=0).astype(jnp.float32)
    rel = jnp.take(relations, kind, axis=0)
    hre, him = (head[:, :half], head[:, half:])
    rre, rim = (rel[:, :half], rel[:, half:])
    query = jnp.concatenate([hre * rre - him * rim, hre * rim + him * rre], axis=1)
    q_low = query.astype(jnp.bfloat16)
    pos = jnp.sum(query * tail, axis=1)
    negrows = jnp.take(right_blk, neg, axis=0)
    scores = lax.dot_general(
        q_low, negrows, (((1,), (1,)), ((), ())), preferred_element_type=jnp.float32
    )
    c_pos = -jax.nn.sigmoid(-pos) * live
    c_neg = (jax.nn.sigmoid(scores) * (live[:, None] / neg.shape[0])).astype(jnp.bfloat16)
    g_query = jnp.dot(c_neg, negrows, preferred_element_type=jnp.float32) + c_pos[:, None] * tail
    g_neg = lax.dot_general(
        c_neg, q_low, (((0,), (0,)), ((), ())), preferred_element_type=jnp.float32
    )
    g_tail = c_pos[:, None] * query
    gre, gim = (g_query[:, :half], g_query[:, half:])
    grad_h = jnp.concatenate([gre * rre + gim * rim, -gre * rim + gim * rre], axis=1)
    grad_r = jnp.concatenate([gre * hre + gim * him, -gre * him + gim * hre], axis=1)
    return (grad_h, grad_r, g_tail, g_neg)


def shards(
    left_table,
    right_table,
    relations,
    source_ids,
    relation_ids,
    target_ids,
    negative_ids,
    edge_counts,
):
    right_blk = right_table[0]
    src_all = source_ids[0, 0]
    kind_all = relation_ids[0, 0]
    dst_all = target_ids[0, 0]
    negs = negative_ids[0, 0]
    count = edge_counts[0, 0]
    blocks = negs.shape[0]
    width = src_all.shape[0] // blocks
    live_blocks = (count + width - 1) // width

    def one(index, carry):
        lgrad, rgrad, tgrad = carry
        start = index * width
        n = lax.dynamic_index_in_dim(negs, index, 0, keepdims=False)
        live = (start + jnp.arange(width, dtype=jnp.int32) < count).astype(jnp.float32)
        grad_h, grad_r, g_tail, g_neg = block_terms(
            left_table, right_blk, relations, src_all, kind_all, dst_all, n, live
        )
        lgrad = lgrad.at[src_all].add(grad_h)
        rgrad = rgrad.at[kind_all].add(grad_r)
        tgrad = tgrad.at[dst_all].add(g_tail).at[n].add(g_neg)
        return (lgrad, rgrad, tgrad)

    init = (
        jnp.zeros(left_table.shape, jnp.float32),
        jnp.zeros(relations.shape, jnp.float32),
        jnp.zeros(right_blk.shape, jnp.float32),
    )
    left_grad, rel_grad, right_grad = lax.fori_loop(0, live_blocks, one, init)
    updated = (right_blk.astype(jnp.float32) - step_size * right_grad).astype(jnp.bfloat16)
    moved = passed_along(updated, "right", 1)
    left_share = lax.psum_scatter(left_grad, "right", scatter_dimension=0, tiled=True)
    rel_total = lax.psum(rel_grad, ("left", "right"))
    rows = left_share.shape[0]
    own_rows = lax.dynamic_slice_in_dim(left_table, lax.axis_index("right") * rows, rows, 0)
    piece = (own_rows.astype(jnp.float32) - step_size * left_share).astype(jnp.bfloat16)
    left_next = lax.all_gather(piece, "right", axis=0, tiled=True)
    relations_next = relations - relation_step * rel_total
    return (left_next, moved[None], relations_next)


def solution(mesh):
    return jax.shard_map(
        shards,
        mesh=mesh,
        in_specs=(
            P("left", None),
            P("left", "right", None),
            P(),
            P("left", "right", None),
            P("left", "right", None),
            P("left", "right", None),
            P("left", "right", None, None),
            P("left", "right"),
        ),
        out_specs=(P("left", None), P("left", "right", None), P()),
        check_vma=False,
    )
```

profile of v0, /device:TPU:0, one launch (start us, length us, event | category | flops | bytes accessed | tf_op | source)
XLA Modules:
  0.0 265.6 jit_solution(17051834910736754311)
XLA Ops:
  8.0 0.0 reduce-scatter.2.cloned.1.call-start
  8.7 0.7 compare_and_fusion.4
  9.4 0.7 fusion.13
  10.1 0.7 compare_select_fusion.9
  10.8 0.7 compare_and_fusion.6
  11.5 0.7 compare_select_fusion.8
  12.2 0.7 compare_and_fusion.5
  12.9 0.0 copy-start
  12.9 4.9 %gather_fusion.4 = bf16[1024,256]{1,0:T(8,128)(2,1)S(1)} fusion(bf16[2048,256]{1,0:T(8,128)(2,1)} %param.12, s32[1024]{0:T(1024)S(1)} %broadcast_clamp_fusion.3), kind=kCustom, calls=%fused_computation.5 | custom fusion | bytes 1052672 | tf_op jit(solution)/shard_map/while/body/jit(_take)/gather | solution.py:17
  17.8 0.0 copy-start.1
  17.8 3.9 %gather_fusion.6 = bf16[1024,256]{1,0:T(8,128)(2,1)S(1)} fusion(bf16[512,256]{1,0:T(8,128)(2,1)S(1)} %bitcast.49, s32[1024]{0:T(1024)S(1)} %fusion.13), kind=kCustom, calls=%fused_computation.4.clone | custom fusion | bytes 1052672 | tf_op jit(solution)/shard_map/while/body/jit(_take)/gather | solution.py:18
  21.7 0.2 select_convert_fusion.1
  22.0 3.5 %gather_fusion.5 = f32[1024,256]{1,0:T(8,128)S(1)} fusion(f32[512,256]{1,0:T(8,128)S(1)} %copy-done.1, s32[1024]{0:T(1024)S(1)} %broadcast_clamp_fusion.2), kind=kCustom, calls=%fused_computation.6 | custom fusion | bytes 2101248 | tf_op jit(solution)/shard_map/while/body/jit(_take)/gather | solution.py:19
  25.4 0.2 broadcast_select_fusion.4
  25.6 0.1 multiply_subtract_fusion.2
  25.8 0.0 copy-start.10
  25.8 0.0 copy-start.11
  25.8 0.4 fusion.12
  26.3 1.5 broadcast_in_dim.66
  27.8 80.1 %while.17 = (s32[]{:T(128)}, f32[2048,256]{1,0:T(8,128)}, f32[512,256]{1,0:T(8,128)S(1)}, f32[512,256]{1,0:T(8,128)S(1)}, s32[]{:T(128)}, /*index=5*/s32[1024]{0...) while((s32[]{:T(128)}, f32[2048,256]{1,0:T(8,128)}, ...), condition=%wide.region_6.8_spmd, body=%wide.region_1.7_spmd.sunk | while | flops 1624953856 | bytes 75646288 | solution.py:80
  28.2 0.7 negate_select_fusion.2
  28.8 5.0 %gather_fusion = bf16[1024,256]{1,0:T(8,128)(2,1)} fusion(bf16[512,256]{1,0:T(8,128)(2,1)S(1)} %get-tuple-element.418, s32[1024]{0:T(1024)S(1)} %fusion.28), kind=kCustom, calls=%fused_computation.clone.clone.1 | custom fusion | bytes 1052672 | tf_op jit(solution)/shard_map/while/body/jit(_take)/gather | solution.py:25
  33.8 3.9 %gather_fusion.3 = bf16[1024,256]{1,0:T(8,128)(2,1)S(1)} fusion(bf16[512,256]{1,0:T(8,128)(2,1)S(1)} %get-tuple-element.418, s32[1024]{0:T(1024)S(1)} %fusion.29), kind=kCustom, calls=%fused_computation.1.clone.clone.1 | custom fusion | bytes 1052672 | tf_op jit(solution)/shard_map/while/body/jit(_take)/gather | solution.py:18
  37.7 1.0 copy.28
  38.8 5.0 %gather_fusion.2 = bf16[1024,256]{1,0:T(8,128)(2,1)} fusion(bf16[2048,256]{1,0:T(8,128)(2,1)S(1)} %get-tuple-element.414, s32[1024]{0:T(1024)S(1)} %broadcast_clamp_fusion.7), kind=kCustom, calls=%fused_computation.2.clone.1 | custom fusion | bytes 1052672 | tf_op jit(solution)/shard_map/while/body/jit(_take)/gather | solution.py:17
  43.8 1.2 copy.27
  45.0 1.1 select_convert_fusion.3
  46.1 4.7 %gather_fusion.1 = f32[1024,256]{1,0:T(8,128)} fusion(f32[512,256]{1,0:T(8,128)S(1)} %get-tuple-element.416, s32[1024]{0:T(1024)S(1)} %broadcast_clamp_fusion.6), kind=kCustom, calls=%fused_computation.3.clone.1 | custom fusion | bytes 2101248 | tf_op jit(solution)/shard_map/while/body/jit(_take)/gather | solution.py:19
  50.7 2.6 copy.26
  53.3 1.4 broadcast_select_fusion.10
  54.7 0.1 copy-done.4
  54.8 0.2 multiply_subtract_fusion.4
  55.1 0.7 copy-done.5
  55.8 0.8 copy-done.6
  56.6 1.1 fusion.30
  57.7 2.5 copy.31
  60.2 6.7 %scatter_fusion.2 = f32[512,256]{1,0:T(8,128)S(1)} fusion(f32[512,256]{1,0:T(8,128)S(1)} %get-tuple-element.395, s32[1024]{0:T(1024)S(1)} %bitcast.70, f32[1024,256]{1,0:T(8,128)} %copy.31), kind=kCustom, calls=%fused_computation.9.clone.1 | custom fusion | flops 262144 | bytes 3149824 | tf_op jit(solution)/shard_map/while/body/scatter-add | solution.py:72
  67.0 0.0 copy-start.9
  67.0 3.0 %multiply_convert_fusion.2 = bf16[1024,1024]{1,0:T(8,128)(2,1)S(1)} fusion(f32[1024]{0:T(1024)S(1)} %get-tuple-element.366, bf16[1024,256]{1,0:T(8,128)(2,1)} %gather_fusion, pred[1024]{0:T(1024)(128)(4,1)S(1)} %compare_and_fusion.10, f32[1024,128]{0,1:T(8,128)} %copy-done.6, f32[1024,128]{0,1:T(8,128)S(1)} %get-tuple-element.369), kind=kOutput, calls=%fused_computation.11.clone.1 | convolution fusion | flops 543424512 | bytes 3675136 | tf_op jit(solution)/shard_map/while/body/dot_general | solution.py:26
  70.0 1.8 convolution_add_fusion.2
  71.8 1.7 fusion.31
  73.5 6.7 %scatter_fusion.3 = f32[512,256]{1,0:T(8,128)S(1)} fusion(f32[512,256]{1,0:T(8,128)S(1)} %scatter_fusion.2, s32[1024]{0:T(1024)S(1)} %bitcast.69, f32[1024,256]{1,0:T(8,128)} %fusion.31), kind=kCustom, calls=%fused_computation.10.clone.1 | custom fusion | flops 262144 | bytes 3149824 | tf_op jit(solution)/shard_map/while/body/scatter-add | solution.py:72
  80.3 3.0 %multiply_add_fusion.7 = (f32[1024,128]{0,1:T(8,128)S(1)}, f32[1024,128]{0,1:T(8,128)}, f32[1024,128]{0,1:T(8,128)S(1)}, f32[1024,128]{0,1:T(8,128)S(1)}) fusion(f32[1024,256]{0,1:T(8,128)} %convolution_add_fusion.2, f32[1024,256]{0,1:T(8,128)} %select_convert_fusion.3, f32[1024,256]{0,1:T(8,128)} %copy-done.5), kind=kLoop, calls=%fused_computation.19.clone.1 | loop fusion | flops 1703936 | bytes 5242880 | tf_op jit(solution)/shard_map/while/body/add | solution.py:38
  83.3 1.0 pad_maximum_fusion.5
  84.3 2.5 copy.29
  86.9 9.4 %scatter_fusion = f32[2048,256]{1,0:T(8,128)} fusion(f32[2048,256]{1,0:T(8,128)} %get-tuple-element.393, s32[1024]{0:T(1024)S(1)} %bitcast.59, f32[1024,256]{1,0:T(8,128)} %copy.29), kind=kCustom, calls=%fused_computation.7.clone.1 | custom fusion | flops 262144 | bytes 3149824 | tf_op jit(solution)/shard_map/while/body/scatter-add | solution.py:70
  96.3 2.1 pad_maximum_fusion.6
  98.4 2.5 copy.30
  100.9 6.7 %scatter_fusion.1 = f32[512,256]{1,0:T(8,128)S(1)} fusion(f32[512,256]{1,0:T(8,128)S(1)} %get-tuple-element.394, s32[1024]{0:T(1024)S(1)} %bitcast.57, f32[1024,256]{1,0:T(8,128)} %copy.30), kind=kCustom, calls=%fused_computation.8.clone.1 | custom fusion | flops 262144 | bytes 3149824 | tf_op jit(solution)/shard_map/while/body/scatter-add | solution.py:71
  107.9 0.0 copy-start.2
  107.9 0.0 reduce-scatter.2.cloned.1.call-update
  108.0 0.0 all-reduce.2.cloned.1.call-start
  108.0 0.7 copy-done.2
  108.7 0.0 all-reduce.2.cloned.1.call-update
  108.7 0.0 all-gather.2.cloned.1.call-start
  108.8 70.6 %reduce-scatter.2.cloned.1.call-done = f32[256,256]{1,0:T(8,128)} async-done(((f32[2048,256]{1,0:T(8,128)}), f32[256,256]{1,0:T(8,128)}) %reduce-scatter.2.cloned.1.call-update) | async-done | bytes 262160 | tf_op jit(solution)/shard_map/reduce_scatter | solution.py:83
  179.4 1.6 subtract_convert_fusion.1
  181.1 0.0 all-gather.2.cloned.1.call-update
  181.1 0.1 subtract_convert_fusion
  181.2 0.9 collective-permute-start
  182.1 71.2 %all-reduce.2.cloned.1.call-done = f32[512,256]{1,0:T(8,128)} async-done(((f32[512,256]{1,0:T(8,128)}), f32[512,256]{1,0:T(8,128)}) %all-reduce.2.cloned.1.call-update) | async-done | bytes 524304 | tf_op jit(solution)/shard_map/psum | solution.py:84
  253.3 1.9 multiply_subtract_fusion.1
  255.2 2.3 copy.52
  257.5 0.7 copy.53
  (36 shorter events, 0.2 us)
Async XLA Ops:
  8.0 171.4 %reduce-scatter.2.cloned.1.call-start = ((), (), s32[]{:S(2)}) async-start(), calls=%async_computation.1 | async-start | bytes 2359296 | tf_op jit(solution)/shard_map/reduce_scatter | solution.py:83
  12.9 4.9 %copy-start = (bf16[1,512,256]{2,1,0:T(8,128)(2,1)S(1)}, bf16[1,512,256]{2,1,0:T(8,128)(2,1)}, u32[]{:S(2)}) copy-start(bf16[1,512,256]{2,1,0:T(8,128)(2,1)} %param.13) | copy-start | bytes 786436
  17.8 4.2 %copy-start.1 = (f32[512,256]{1,0:T(8,128)S(1)}, f32[512,256]{1,0:T(8,128)}, u32[]{:S(2)}) copy-start(f32[512,256]{1,0:T(8,128)} %param.14) | copy-start | bytes 1572868
  25.8 2.0 copy-start.3
  25.8 2.0 copy-start.10
  25.8 2.0 copy-start.11
  25.8 2.0 copy-start.12
  25.8 2.0 copy-start.13
  53.3 1.5 copy-start.4
  54.8 1.0 copy-start.5
  55.8 0.8 copy-start.6
  67.0 3.0 %copy-start.8 = (bf16[1024,256]{0,1:T(8,128)(2,1)S(1)}, bf16[1024,256]{0,1:T(8,128)(2,1)}, u32[]{:S(2)}) copy-start(bf16[1024,256]{0,1:T(8,128)(2,1)} %copy.28) | copy-start | bytes 1572868 | tf_op jit(solution)/shard_map/while
  67.0 3.0 %copy-start.9 = (bf16[1024,256]{1,0:T(8,128)(2,1)S(1)}, bf16[1024,256]{1,0:T(8,128)(2,1)}, u32[]{:S(2)}) copy-start(bf16[1024,256]{1,0:T(8,128)(2,1)} %gather_fusion) | copy-start | bytes 1572868 | tf_op jit(solution)/shard_map/while
  70.0 1.8 copy-start.7
  107.9 0.8 copy-start.2
  108.0 145.3 %all-reduce.2.cloned.1.call-start = ((), (), s32[]{:S(2)}) async-start(), calls=%async_computation.3 | async-start | bytes 1048576 | tf_op jit(solution)/shard_map/psum | solution.py:84
  108.7 146.5 %all-gather.2.cloned.1.call-start = ((), (), s32[]{:S(2)}) async-start(), calls=%async_computation.2 | async-start | bytes 1179648 | tf_op jit(solution)/shard_map/all_gather | solution.py:88
  181.2 74.0 %collective-permute-start = (bf16[512,256]{1,0:T(8,128)(2,1)S(1)}, bf16[512,256]{1,0:T(8,128)(2,1)S(1)}, u32[]{:S(2)}, u32[]{:S(2)}) collective-permute-start(bf16[512,256]{1,0:T(8,128)(2,1)S(1)} %subtract_convert_fusion), channel_id=1, source_target_pairs={{0,1},{1,2},{2,3},{3,4},{4,5},{5,6},{6,7},{7,0},{8,9},{9,10},{10,1... | collective-permute-start | bytes 786440 | tf_op jit(solution)/shard_map/ppermute | solution.py:12
Sparse Core Ops, SparseCore 0:
  108.1 71.3 reduce-scatter.1
  182.1 39.4 all-gather.1
Sparse Core Ops, SparseCore 1:
  114.3 139.0 all-reduce.1
where the time goes:
time: 267 us; the launch traced here: 266 us
  waiting for transfers between devices  142 us (53%)
  local copies, waits for them, and re-layouts  50.2 us (19%)
  other arithmetic  48.9 us (18%)
  between operations  16.4 us (6%)
  matrix products  6.52 us (2%)
    psum x1, waiting for transfers between devices, shards(): rel_total = lax.psum(rel_grad, ('left', 'right'))  71.2 us
    reduce_scatter x1, waiting for transfers between devices, shards(): lax.psum_scatter(left_grad, 'right', scatter_dimension=0, tiled=True)  70.6 us
    scatter-add x2, other arithmetic, one(): tgrad = tgrad.at[dst_all].add(g_tail).at[n].add(g_neg)  13.5 us
    gather x3, local copies, waits for them, and re-layouts, block_terms(): head = jnp.take(left_blk, src, axis=0).astype(jnp.float32)  11.1 us
    gather x3, local copies, waits for them, and re-layouts, block_terms(): rel = jnp.take(relations, kind, axis=0)  10.7 us
    scatter-add x1, other arithmetic, one(): lgrad = lgrad.at[src_all].add(grad_h)  9.4 us
    gather x3, local copies, waits for them, and re-layouts, block_terms(): tail = jnp.take(right_blk, dst, axis=0).astype(jnp.float32)  8.91 us
    scatter-add x1, other arithmetic, one(): rgrad = rgrad.at[kind_all].add(grad_r)  6.74 us
  transfers between devices with their start and end apart: 4, of which 2 were waited for; matrix products, arithmetic and copies ran while one was open for 1% of the time, Pallas kernels for 0%

commit v1 on v0

v1 whole, which is shorter than its diff:
```python
import functools

import jax
import jax.numpy as jnp
from jax import lax
from jax.experimental import pallas as pl
from jax.experimental.pallas import tpu as pltpu
from jax.sharding import PartitionSpec as P

step_size = 0.5
relation_step = 12.0

f32, bf16 = jnp.float32, jnp.bfloat16
VMEM = pltpu.VMEM


def split(value):
    high = value.astype(bf16)
    low = (value - high.astype(f32)).astype(bf16)
    return jnp.concatenate([high, low], axis=1)


def joined(value):
    half = value.shape[1] // 2
    return value[:, :half] + value[:, half:]


def matmul(a, b, dims=((1,), (0,))):
    return lax.dot_general(a, b, (dims, ((), ())), preferred_element_type=f32)


def one_hot(ids, shape, axis):
    place = lax.broadcasted_iota(jnp.int32, shape, axis)
    return jnp.where(place == ids, 1.0, 0.0).astype(bf16)


def terms_kernel(
    count_ref, left_ref, right_ref, rel_ref, src_ref, kind_ref, dst_ref, neg_ref,
    lgrad_ref, rgrad_ref, updated_ref,
    rows_ref, cols_ref, rel_parts, neg_parts, heads, kinds, tails, low_ref, weights,
):
    edges = src_ref.shape[1]
    ent_l, width = left_ref.shape
    ent_r = right_ref.shape[0]
    rels = rel_ref.shape[0]
    negs = neg_ref.shape[1]
    half = width // 2
    block = min(256, edges)

    rows_ref[...] = jnp.zeros_like(rows_ref)
    rows_ref[0:1, :] = src_ref[...]
    rows_ref[1:2, :] = kind_ref[...]
    rows_ref[2:3, :] = dst_ref[...]
    cols_ref[...] = jnp.transpose(rows_ref[...])
    rel_parts[...] = split(rel_ref[...])
    place = lax.broadcasted_iota(jnp.int32, (ent_r, negs), 0)
    times = jnp.sum(jnp.where(place == neg_ref[...], 1.0, 0.0), axis=1, keepdims=True)
    neg_parts[...] = split(right_ref[...].astype(f32) * times)
    count = count_ref[0, 0]

    @pl.loop(0, edges // block)
    def _(step):
        start = pl.multiple_of(step * block, block)
        here = pl.ds(start, block)
        ids = cols_ref[here, :]
        head = matmul(one_hot(ids[:, 0:1], (block, ent_l), 1), left_ref[...])
        rel = joined(matmul(one_hot(ids[:, 1:2], (block, rels), 1), rel_parts[...]))
        tail = matmul(one_hot(ids[:, 2:3], (block, ent_r), 1), right_ref[...])
        slot = start + lax.broadcasted_iota(jnp.int32, (block, 1), 0)
        live = jnp.where(slot < count, 1.0, 0.0)
        hre, him = head[:, :half], head[:, half:]
        rre, rim = rel[:, :half], rel[:, half:]
        query = jnp.concatenate([hre * rre - him * rim, hre * rim + him * rre], axis=1)
        q_low = query.astype(bf16)
        pos = jnp.sum(query * tail, axis=1, keepdims=True)
        scores = matmul(q_low, right_ref[...], ((1,), (1,)))
        c_pos = -live / (1.0 + jnp.exp(pos))
        c_neg = ((live / negs) / (1.0 + jnp.exp(-scores))).astype(bf16)
        g_query = joined(matmul(c_neg, neg_parts[...])) + c_pos * tail
        gre, gim = g_query[:, :half], g_query[:, half:]
        heads[here, :] = split(
            jnp.concatenate([gre * rre + gim * rim, -gre * rim + gim * rre], axis=1)
        )
        kinds[here, :] = split(
            jnp.concatenate([gre * hre + gim * him, -gre * him + gim * hre], axis=1)
        )
        tails[here, :] = split(c_pos * query)
        low_ref[here, :] = q_low
        weights[here, :] = c_neg

    def summed(ids_row, rows, parts, store):
        size = min(256, rows)

        @pl.loop(0, rows // size)
        def _(step):
            start = pl.multiple_of(step * size, size)
            hot = one_hot(ids_row[...] - start, (size, edges), 0)
            store(start, size, joined(matmul(hot, parts[...])))

    def store_left(start, size, value):
        lgrad_ref[pl.ds(start, size), :] = value

    def store_rel(start, size, value):
        rgrad_ref[pl.ds(start, size), :] = value

    grad = matmul(weights[...], low_ref[...], ((0,), (0,))) * times
    hot = one_hot(dst_ref[...], (ent_r, edges), 0)
    grad = grad + joined(matmul(hot, tails[...]))
    updated_ref[...] = (right_ref[...].astype(f32) - step_size * grad).astype(bf16)
    summed(kind_ref, rels, kinds, store_rel)
    summed(src_ref, ent_l, heads, store_left)


def terms(left, right, relations, src, kind, dst, neg, count):
    edges = src.shape[1]
    ent_l, width = left.shape
    ent_r, rels = right.shape[0], relations.shape[0]
    whole = pl.BlockSpec(memory_space=VMEM)
    return pl.pallas_call(
        terms_kernel,
        out_shape=(
            jax.ShapeDtypeStruct((ent_l, width), f32),
            jax.ShapeDtypeStruct((rels, width), f32),
            jax.ShapeDtypeStruct((ent_r, width), bf16),
        ),
        in_specs=[pl.BlockSpec(memory_space=pltpu.SMEM)] + [whole] * 7,
        out_specs=(whole,) * 3,
        scratch_shapes=[
            VMEM((8, edges), jnp.int32),
            VMEM((edges, 8), jnp.int32),
            VMEM((rels, 2 * width), bf16),
            VMEM((ent_r, 2 * width), bf16),
            VMEM((edges, 2 * width), bf16),
            VMEM((edges, 2 * width), bf16),
            VMEM((edges, 2 * width), bf16),
            VMEM((edges, width), bf16),
            VMEM((edges, ent_r), bf16),
        ],
        compiler_params=pltpu.CompilerParams(vmem_limit_bytes=44 * 2**20),
        name="bucket_terms",
    )(count, left, right, relations, src, kind, dst, neg)


def exchange_kernel(
    nl, nr,
    lgrad_ref, rgrad_ref, block_ref, left_ref, rel_ref,
    left_out, block_out, rel_out,
    pair_in, line_in, rel_in, rel_mid, rel_part,
    block_sems, pair_send, pair_recv, line_send, line_recv,
    rows_send, rows_recv, back_send, back_recv,
    ra_send, ra_recv, rb_send, rb_recv, rc_send, rc_recv, rd_send, rd_recv,
):
    m = nr // 2
    l, r = lax.axis_index("left"), lax.axis_index("right")
    line, side = r // 2, lax.rem(r, 2)
    mate = line * 2 + (1 - side)

    def across(src, dst, send, recv, axis, to):
        return pltpu.make_async_remote_copy(
            src_ref=src, dst_ref=dst, send_sem=send, recv_sem=recv,
            device_id={axis: to}, device_id_type=pl.DeviceIdType.MESH,
        )

    def others(me, count):
        return [lax.rem(me + k, count) for k in range(1, count)]

    lefts, rights, lines = others(l, nl), others(r, nr), others(line, m)

    barrier = pltpu.get_barrier_semaphore()
    for axis, peers in (("left", lefts), ("right", rights)):
        for peer in peers:
            pl.semaphore_signal(
                barrier, inc=1, device_id={axis: peer},
                device_id_type=pl.DeviceIdType.MESH,
            )
    pl.semaphore_wait(barrier, nl - 1 + nr - 1)

    started = []

    def start(*what):
        copy = across(*what)
        copy.start()
        started.append(copy)

    for peer in lefts:
        start(rgrad_ref.at[peer], rel_in.at[l], ra_send.at[peer], ra_recv.at[l], "left", peer)
    order = lines + [line]
    for j in order:
        start(
            lgrad_ref.at[1 - side, j], pair_in.at[j], pair_send.at[j], pair_recv.at[j],
            "right", mate,
        )
    after = lax.rem(r + 1, nr)
    start(block_ref, block_out, block_sems.at[0], block_sems.at[1], "right", after)

    def arrived(dst, sem, axis="right"):
        across(dst, dst, sem, sem, axis, mate if axis == "right" else lefts[0]).wait_recv()

    total = rgrad_ref[l]
    for peer in lefts:
        arrived(rel_in.at[peer], ra_recv.at[peer], "left")
        total = total + rel_in[peer]
    rel_part[...] = total
    for peer in rights:
        start(rel_part.at[peer], rel_mid.at[r], rb_send.at[peer], rb_recv.at[r], "right", peer)

    for j in order:
        arrived(pair_in.at[j], pair_recv.at[j])
        pair_in[j] = pair_in[j] + lgrad_ref[side, j]
        if j is not line:
            start(
                pair_in.at[j], line_in.at[line], line_send.at[j], line_recv.at[line],
                "right", j * 2 + side,
            )

    total = rel_part[r]
    for peer in rights:
        arrived(rel_mid.at[peer], rb_recv.at[peer])
        total = total + rel_mid[peer]
    rel_out[l, r] = rel_ref[l, r] - relation_step * total
    for peer in rights:
        start(rel_out.at[l, r], rel_out.at[l, r], rc_send.at[peer], rc_recv.at[r], "right", peer)

    total = pair_in[line]
    for j in lines:
        arrived(line_in.at[j], line_recv.at[j])
        total = total + line_in[j]
    left_out[side, line] = (
        left_ref[side, line].astype(f32) - step_size * total
    ).astype(bf16)
    own = left_out.at[side, line]
    for j in lines:
        start(own, own, rows_send.at[j], rows_recv.at[line], "right", j * 2 + side)
    start(own, own, back_send.at[line], back_recv.at[line], "right", mate)

    for peer in rights:
        arrived(rel_out.at[l, peer], rc_recv.at[peer])
    for peer in lefts:
        start(rel_out.at[l], rel_out.at[l], rd_send.at[peer], rd_recv.at[l], "left", peer)

    for j in lines:
        piece = left_out.at[side, j]
        arrived(piece, rows_recv.at[j])
        start(piece, piece, back_send.at[j], back_recv.at[j], "right", mate)
    for j in order:
        arrived(left_out.at[1 - side, j], back_recv.at[j])
    for peer in lefts:
        arrived(rel_out.at[peer], rd_recv.at[peer], "left")
    arrived(block_out, block_sems.at[1])
    for copy in started:
        copy.wait_send()


def exchange(nl, nr, lgrad, rgrad, block, left, relations):
    m = nr // 2
    ent_l, width = left.shape
    rels = relations.shape[0]
    piece, part, share = ent_l // nr, rels // nl, rels // (nl * nr)
    whole = pl.BlockSpec(memory_space=VMEM)
    dma = pltpu.SemaphoreType.DMA
    left_next, moved, relations_next = pl.pallas_call(
        functools.partial(exchange_kernel, nl, nr),
        out_shape=(
            jax.ShapeDtypeStruct((2, m, piece, width), bf16),
            jax.ShapeDtypeStruct(block.shape, bf16),
            jax.ShapeDtypeStruct((nl, nr, share, width), f32),
        ),
        in_specs=[whole] * 5,
        out_specs=(whole,) * 3,
        scratch_shapes=[
            VMEM((m, piece, width), f32),
            VMEM((m, piece, width), f32),
            VMEM((nl, nr, share, width), f32),
            VMEM((nr, share, width), f32),
            VMEM((nr, share, width), f32),
            dma((2,)),
        ] + [dma((m,))] * 8 + [dma((nl,))] * 2 + [dma((nr,))] * 4 + [dma((nl,))] * 2,
        compiler_params=pltpu.CompilerParams(
            collective_id=0, has_side_effects=True, vmem_limit_bytes=44 * 2**20
        ),
        name="exchange",
    )(
        lgrad.reshape(2, m, piece, width),
        rgrad.reshape(nl, nr, share, width),
        block,
        left.reshape(2, m, piece, width),
        relations.reshape(nl, nr, share, width),
    )
    return (
        left_next.reshape(ent_l, width), moved, relations_next.reshape(rels, width),
    )


def solution(mesh):
    nl, nr = mesh.shape["left"], mesh.shape["right"]

    def shards(left, right, relations, src, kind, dst, neg, count):
        lgrad, rgrad, block = terms(
            left, right[0], relations, src[0], kind[0], dst[0], neg[0, 0], count
        )
        left_next, moved, relations_next = exchange(
            nl, nr, lgrad, rgrad, block, left, relations
        )
        return (left_next, moved[None], relations_next)

    return jax.shard_map(
        shards,
        mesh=mesh,
        in_specs=(
            P("left", None),
            P("left", "right", None),
            P(),
            P("left", "right", None),
            P("left", "right", None),
            P("left", "right", None),
            P("left", "right", None, None),
            P("left", "right"),
        ),
        out_specs=(P("left", None), P("left", "right", None), P()),
        check_vma=False,
    )
```

time: 267 us -> 88.1 us (0.33)
  the two profiles are of different devices: /device:TPU:0 before, /device:TPU:12 now
where the time goes in v1:
time: 88.1 us; the launch traced here: 87.7 us
  Pallas kernels  78 us (89%)
  local copies, waits for them, and re-layouts  8.42 us (10%)
  between operations  1.31 us (1%)
    pallas_call x1, Pallas kernels, exchange(): pl.pallas_call(functools.partial(exchange_kernel, nl, nr), out_shape=(jax...  67 us
    pallas_call x1, Pallas kernels, terms(): pl.pallas_call(terms_kernel, out_shape=(jax.ShapeDtypeStruct((ent_l, widt...  11 us
    unnamed x17, local copies, waits for them, and re-layouts  8.42 us

profile of v1, /device:TPU:12, one launch (start us, length us, event | category | flops | bytes accessed | tf_op | source)
XLA Modules:
  0.0 87.7 jit_solution(6548263723428930681)
XLA Ops:
  1.3 0.0 copy-start
  1.3 1.2 %copy-done = bf16[2048,256]{1,0:T(8,128)(2,1)S(1)} copy-done((bf16[2048,256]{1,0:T(8,128)(2,1)S(1)}, bf16[2048,256]{1,0:T(8,128)(2,1)}, u32[]{:S(2)}) %copy-start) | copy-done | bytes 1048600
  2.5 0.0 copy-start.1
  2.5 1.0 %copy-done.1 = f32[512,256]{1,0:T(8,128)S(1)} copy-done((f32[512,256]{1,0:T(8,128)S(1)}, f32[512,256]{1,0:T(8,128)}, u32[]{:S(2)}) %copy-start.1) | copy-done | bytes 524312
  3.5 0.0 copy-start.2
  3.5 0.9 %copy-done.2 = bf16[1,512,256]{2,1,0:T(8,128)(2,1)S(1)} copy-done((bf16[1,512,256]{2,1,0:T(8,128)(2,1)S(1)}, bf16[1,512,256]{2,1,0:T(8,128)(2,1)}, u32[]{:S(2)}) %copy-start.2) | copy-done | bytes 262168
  4.5 0.0 copy-start.3
  4.5 0.7 copy-done.3
  5.2 0.0 copy-start.4
  5.2 0.7 copy-done.4
  5.9 0.0 copy-start.5
  5.9 0.7 copy-done.5
  6.6 0.0 copy-start.6
  6.6 0.7 copy-done.6
  7.2 11.0 %bucket_terms.1 = (f32[2048,256]{1,0:T(8,128)S(1)}, f32[512,256]{1,0:T(8,128)S(1)}, bf16[512,256]{1,0:T(8,128)(2,1)S(1)}) custom-call(s32[1,1]{1,0:T(1,128)S(6)} %copy.14.count_ref, bf16[2048,256]{1,0:T(8,128)(2,1)S(1)} %copy-done, bf16[512,256]{1,0:T(8,128)(2,1)S(1)} %bitcast.19, f32[512,256]{1,0:T(8,128)S(1)} %copy-done.1, s32[1,1024]{1,0:T(1,128)S(1)} %bitcast.20, ...), custom_call_target="tpu_custom_call" | custom-call | tf_op jit(solution)/shard_map/bucket_terms/pallas_call | solution.py:119
  18.3 67.0 %exchange.1 = (bf16[2,4,256,256]{3,2,1,0:T(8,128)(2,1)S(1)}, bf16[512,256]{1,0:T(8,128)(2,1)S(1)}, f32[4,8,16,256]{3,2,1,0:T(8,128)S(1)}) custom-call(f32[2,4,256,256]{3,2,1,0:T(8,128)S(1)} %bitcast.13, f32[4,8,16,256]{3,2,1,0:T(8,128)S(1)} %bitcast.16, bf16[512,256]{1,0:T(8,128)(2,1)S(1)} %get-tuple-element.11.block_ref, ...), custom_call_target="tpu_custom_call" | custom-call | tf_op jit(solution)/shard_map/exchange/pallas_call | solution.py:261
  85.2 1.0 %copy.15 = bf16[2048,256]{1,0:T(8,128)(2,1)} copy(bf16[2048,256]{1,0:T(8,128)(2,1)S(1)} %bitcast.15) | data formatting | bytes 2097152
  86.2 0.7 copy.16
  86.9 0.8 copy.17
Async XLA Ops:
  1.3 1.2 %copy-start = (bf16[2048,256]{1,0:T(8,128)(2,1)S(1)}, bf16[2048,256]{1,0:T(8,128)(2,1)}, u32[]{:S(2)}) copy-start(bf16[2048,256]{1,0:T(8,128)(2,1)} %left_ref.1) | copy-start | bytes 3145732
  2.5 1.0 %copy-start.1 = (f32[512,256]{1,0:T(8,128)S(1)}, f32[512,256]{1,0:T(8,128)}, u32[]{:S(2)}) copy-start(f32[512,256]{1,0:T(8,128)} %rel_ref.1) | copy-start | bytes 1572868
  3.5 0.9 %copy-start.2 = (bf16[1,512,256]{2,1,0:T(8,128)(2,1)S(1)}, bf16[1,512,256]{2,1,0:T(8,128)(2,1)}, u32[]{:S(2)}) copy-start(bf16[1,512,256]{2,1,0:T(8,128)(2,1)} %param.9) | copy-start | bytes 786436
  4.5 0.7 copy-start.3
  5.2 0.7 copy-start.4
  5.9 0.7 copy-start.5
  6.6 0.7 copy-start.6

commit v2 on v1

v2 whole, which is shorter than its diff:
```python
import functools

import jax
import jax.numpy as jnp
from jax import lax
from jax.experimental import pallas as pl
from jax.experimental.pallas import tpu as pltpu
from jax.sharding import PartitionSpec as P

step_size = 0.5
relation_step = 12.0

f32, bf16 = jnp.float32, jnp.bfloat16
VMEM = pltpu.VMEM


def split(value):
    high = value.astype(bf16)
    low = (value - high.astype(f32)).astype(bf16)
    return jnp.concatenate([high, low], axis=1)


def joined(value):
    half = value.shape[1] // 2
    return value[:, :half] + value[:, half:]


def matmul(a, b, dims=((1,), (0,))):
    return lax.dot_general(a, b, (dims, ((), ())), preferred_element_type=f32)


def one_hot(ids, shape, axis):
    place = lax.broadcasted_iota(jnp.int32, shape, axis)
    return jnp.where(place == ids, 1.0, 0.0).astype(bf16)


def low_bit(mask):
    return (mask & -mask).bit_length() - 1


def flip(value, mask):
    bit = 1
    while bit <= mask:
        if mask & bit:
            value = value + bit * (1 - 2 * lax.rem(value // bit, 2))
        bit *= 2
    return value


def round_kernel(
    nl, nr,
    count_ref, left_any, right_any, rel_any, src_any, kind_any, dst_any, neg_any,
    left_out, block_out, rel_out,
    left_ref, right_ref, rel_ref, src_ref, kind_ref, dst_ref, neg_ref,
    rows_ref, cols_ref, rel_parts, neg_parts, heads, kinds, tails, low_ref, weights,
    block_ref, to_mate, held, pair_in, level_in, rgrad, rel_in, rel_mid, rel_part,
    load_sems, send_sems, block_recv, pair_recv, level_recv, rows_recv, back_recv,
    ra_recv, rb_recv, rc_recv, rd_recv,
):
    m = nr // 2
    levels = m.bit_length() - 1
    edges = src_ref.shape[1]
    ent_l, width = left_ref.shape
    ent_r = right_ref.shape[0]
    share = rel_ref.shape[2]
    rels = nl * nr * share
    negs = neg_ref.shape[1]
    half = width // 2
    piece = ent_l // nr
    block = min(256, edges)
    l, r = lax.axis_index("left"), lax.axis_index("right")
    line, side = r // 2, lax.rem(r, 2)
    mate = line * 2 + (1 - side)

    loads = []
    for i, (src, dst) in enumerate((
        (src_any, src_ref), (kind_any, kind_ref), (dst_any, dst_ref), (neg_any, neg_ref),
        (rel_any, rel_ref), (right_any, right_ref), (left_any, left_ref),
    )):
        load = pltpu.make_async_copy(src, dst, load_sems.at[i])
        load.start()
        loads.append(load)

    def across(src, dst, send, recv, axis, to):
        return pltpu.make_async_remote_copy(
            src_ref=src, dst_ref=dst, send_sem=send, recv_sem=recv,
            device_id={axis: to}, device_id_type=pl.DeviceIdType.MESH,
        )

    def others(me, count):
        return [lax.rem(me + k, count) for k in range(1, count)]

    lefts, rights = others(l, nl), others(r, nr)

    barrier = pltpu.get_barrier_semaphore()
    for axis, peers in (("left", lefts), ("right", rights)):
        for peer in peers:
            pl.semaphore_signal(
                barrier, inc=1, device_id={axis: peer},
                device_id_type=pl.DeviceIdType.MESH,
            )

    for load in loads:
        load.wait()

    rows_ref[...] = jnp.zeros_like(rows_ref)
    rows_ref[0:1, :] = src_ref[...]
    rows_ref[1:2, :] = kind_ref[...]
    rows_ref[2:3, :] = dst_ref[...]
    cols_ref[...] = jnp.transpose(rows_ref[...])
    rel_parts[...] = split(rel_ref[...].reshape(rels, width))
    place = lax.broadcasted_iota(jnp.int32, (ent_r, negs), 0)
    times = jnp.sum(jnp.where(place == neg_ref[...], 1.0, 0.0), axis=1, keepdims=True)
    neg_parts[...] = split(right_ref[...].astype(f32) * times)
    count = count_ref[0, 0]

    @pl.loop(0, edges // block)
    def _(step):
        start = pl.multiple_of(step * block, block)
        here = pl.ds(start, block)
        ids = cols_ref[here, :]
        head = matmul(one_hot(ids[:, 0:1], (block, ent_l), 1), left_ref[...])
        rel = joined(matmul(one_hot(ids[:, 1:2], (block, rels), 1), rel_parts[...]))
        tail = matmul(one_hot(ids[:, 2:3], (block, ent_r), 1), right_ref[...])
        slot = start + lax.broadcasted_iota(jnp.int32, (block, 1), 0)
        live = jnp.where(slot < count, 1.0, 0.0)
        hre, him = head[:, :half], head[:, half:]
        rre, rim = rel[:, :half], rel[:, half:]
        query = jnp.concatenate([hre * rre - him * rim, hre * rim + him * rre], axis=1)
        q_low = query.astype(bf16)
        pos = jnp.sum(query * tail, axis=1, keepdims=True)
        scores = matmul(q_low, right_ref[...], ((1,), (1,)))
        c_pos = -live / (1.0 + jnp.exp(pos))
        c_neg = ((live / negs) / (1.0 + jnp.exp(-scores))).astype(bf16)
        g_query = joined(matmul(c_neg, neg_parts[...])) + c_pos * tail
        gre, gim = g_query[:, :half], g_query[:, half:]
        heads[here, :] = split(
            jnp.concatenate([gre * rre + gim * rim, -gre * rim + gim * rre], axis=1)
        )
        kinds[here, :] = split(
            jnp.concatenate([gre * hre + gim * him, -gre * him + gim * hre], axis=1)
        )
        tails[here, :] = split(c_pos * query)
        low_ref[here, :] = q_low
        weights[here, :] = c_neg

    def summed(ids_row, start, size, parts):
        hot = one_hot(ids_row[...] - start, (size, edges), 0)
        return joined(matmul(hot, parts[...]))

    pl.semaphore_wait(barrier, nl - 1 + nr - 1)

    started = []

    def start(src, dst, recv, axis, to):
        copy = across(src, dst, send_sems.at[len(started)], recv, axis, to)
        copy.start()
        started.append(copy)

    def arrived(dst, sem, axis="right"):
        across(dst, dst, sem, sem, axis, mate if axis == "right" else lefts[0]).wait_recv()

    for peer in lefts:
        rgrad[peer] = summed(kind_ref, peer * (nr * share), nr * share, kinds).reshape(
            nr, share, width
        )
        start(rgrad.at[peer], rel_in.at[l], ra_recv.at[l], "left", peer)

    order = list(range(m - 1, -1, -1))
    spots = [flip(line, k) for k in range(m)]
    for k in order:
        to_mate[k] = summed(src_ref, ((1 - side) * m + spots[k]) * piece, piece, heads)
        start(to_mate.at[k], pair_in.at[k], pair_recv.at[k], "right", mate)

    total = summed(kind_ref, l * (nr * share), nr * share, kinds).reshape(nr, share, width)
    for peer in lefts:
        arrived(rel_in.at[peer], ra_recv.at[peer], "left")
        total = total + rel_in[peer]
    rel_part[...] = total
    for peer in rights:
        start(rel_part.at[peer], rel_mid.at[r], rb_recv.at[r], "right", peer)

    for k in order:
        held[k] = summed(src_ref, (side * m + spots[k]) * piece, piece, heads)

    grad = matmul(weights[...], low_ref[...], ((0,), (0,))) * times
    hot = one_hot(dst_ref[...], (ent_r, edges), 0)
    grad = grad + joined(matmul(hot, tails[...]))
    block_ref[...] = (right_ref[...].astype(f32) - step_size * grad).astype(bf16)
    start(block_ref, block_out, block_recv.at[0], "right", lax.rem(r + 1, nr))

    for k in order:
        arrived(pair_in.at[k], pair_recv.at[k])
        total = held[k] + pair_in[k]
        top = low_bit(k) if k else levels
        for level in range(top):
            arrived(level_in.at[level, k], level_recv.at[level, k])
            total = total + level_in[level, k]
        if k:
            held[k] = total
            there = k - (1 << top)
            start(
                held.at[k], level_in.at[top, there], level_recv.at[top, there],
                "right", spots[1 << top] * 2 + side,
            )
    own_rows = pl.ds(pl.multiple_of((side * m + line) * piece, piece), piece)
    left_out[side, line] = (
        left_ref[own_rows, :].astype(f32) - step_size * total
    ).astype(bf16)

    def pass_on(k):
        rows = left_out.at[side, spots[k]]
        for level in range((low_bit(k) if k else levels) - 1, -1, -1):
            there = k + (1 << level)
            start(rows, rows, rows_recv.at[there], "right", spots[1 << level] * 2 + side)
        start(rows, rows, back_recv.at[k], "right", mate)

    pass_on(0)

    total = rel_part[r]
    for peer in rights:
        arrived(rel_mid.at[peer], rb_recv.at[peer])
        total = total + rel_mid[peer]
    rel_out[l, r] = rel_ref[l, r] - relation_step * total
    for peer in rights:
        start(rel_out.at[l, r], rel_out.at[l, r], rc_recv.at[r], "right", peer)

    later = sorted(range(1, m), key=lambda k: (-low_bit(k), k))
    for k in later[:1]:
        arrived(left_out.at[side, spots[k]], rows_recv.at[k])
        pass_on(k)
    for peer in rights:
        arrived(rel_out.at[l, peer], rc_recv.at[peer])
    for peer in lefts:
        start(rel_out.at[l], rel_out.at[l], rd_recv.at[l], "left", peer)
    for k in later[1:]:
        arrived(left_out.at[side, spots[k]], rows_recv.at[k])
        pass_on(k)

    for k in [0] + later:
        arrived(left_out.at[1 - side, spots[k]], back_recv.at[k])
    for peer in lefts:
        arrived(rel_out.at[peer], rd_recv.at[peer], "left")
    arrived(block_out, block_recv.at[0])
    for copy in started:
        copy.wait_send()


def bucket_round(nl, nr, left, right, relations, src, kind, dst, neg, count):
    m = nr // 2
    levels = max(m.bit_length() - 1, 1)
    edges, negs = src.shape[1], neg.shape[1]
    ent_l, width = left.shape
    ent_r, rels = right.shape[0], relations.shape[0]
    piece, share = ent_l // nr, rels // (nl * nr)
    whole = pl.BlockSpec(memory_space=VMEM)
    outside = pl.BlockSpec(memory_space=pl.ANY)
    dma = pltpu.SemaphoreType.DMA
    sends = 2 * (nl - 1) + 2 * (nr - 1) + 1 + m + (m - 1) + (m - 1) + m
    left_next, moved, relations_next = pl.pallas_call(
        functools.partial(round_kernel, nl, nr),
        out_shape=(
            jax.ShapeDtypeStruct((2, m, piece, width), bf16),
            jax.ShapeDtypeStruct((ent_r, width), bf16),
            jax.ShapeDtypeStruct((nl, nr, share, width), f32),
        ),
        in_specs=[pl.BlockSpec(memory_space=pltpu.SMEM)] + [outside] * 7,
        out_specs=(whole,) * 3,
        scratch_shapes=[
            VMEM((ent_l, width), bf16),
            VMEM((ent_r, width), bf16),
            VMEM((nl, nr, share, width), f32),
            VMEM((1, edges), jnp.int32),
            VMEM((1, edges), jnp.int32),
            VMEM((1, edges), jnp.int32),
            VMEM((1, negs), jnp.int32),
            VMEM((8, edges), jnp.int32),
            VMEM((edges, 8), jnp.int32),
            VMEM((rels, 2 * width), bf16),
            VMEM((ent_r, 2 * width), bf16),
            VMEM((edges, 2 * width), bf16),
            VMEM((edges, 2 * width), bf16),
            VMEM((edges, 2 * width), bf16),
            VMEM((edges, width), bf16),
            VMEM((edges, ent_r), bf16),
            VMEM((ent_r, width), bf16),
            VMEM((m, piece, width), f32),
            VMEM((m, piece, width), f32),
            VMEM((m, piece, width), f32),
            VMEM((levels, m, piece, width), f32),
            VMEM((nl, nr, share, width), f32),
            VMEM((nl, nr, share, width), f32),
            VMEM((nr, share, width), f32),
            VMEM((nr, share, width), f32),
            dma((7,)), dma((sends,)), dma((1,)), dma((m,)), dma((levels, m)),
            dma((m,)), dma((m,)), dma((nl,)), dma((nr,)), dma((nr,)), dma((nl,)),
        ],
        compiler_params=pltpu.CompilerParams(
            collective_id=0, has_side_effects=True, vmem_limit_bytes=44 * 2**20
        ),
        name="bucket_round",
    )(
        count, left, right, relations.reshape(nl, nr, share, width), src, kind, dst, neg,
    )
    return (
        left_next.reshape(ent_l, width), moved, relations_next.reshape(rels, width),
    )


def solution(mesh):
    nl, nr = mesh.shape["left"], mesh.shape["right"]

    def shards(left, right, relations, src, kind, dst, neg, count):
        left_next, moved, relations_next = bucket_round(
            nl, nr, left, right[0], relations, src[0], kind[0], dst[0], neg[0, 0], count
        )
        return (left_next, moved[None], relations_next)

    return jax.shard_map(
        shards,
        mesh=mesh,
        in_specs=(
            P("left", None),
            P("left", "right", None),
            P(),
            P("left", "right", None),
            P("left", "right", None),
            P("left", "right", None),
            P("left", "right", None, None),
            P("left", "right"),
        ),
        out_specs=(P("left", None), P("left", "right", None), P()),
        check_vma=False,
    )
```

time: 88.1 us -> 77.2 us (0.88)
  the two profiles are of different devices: /device:TPU:12 before, /device:TPU:0 now
where the time goes in v2:
time: 77.2 us; the launch traced here: 76.9 us
  Pallas kernels  68.5 us (89%)
  local copies, waits for them, and re-layouts  7.05 us (9%)
  between operations  1.34 us (2%)
    pallas_call x1, Pallas kernels, bucket_round(): pl.pallas_call(functools.partial(round_kernel, nl, nr), out_shape=(jax.Sh...  68.5 us
    unnamed x17, local copies, waits for them, and re-layouts  7.05 us

profile of v2, /device:TPU:0, one launch (start us, length us, event | category | flops | bytes accessed | tf_op | source)
XLA Modules:
  0.0 76.9 jit_solution(11954917307974618327)
XLA Ops:
  0.6 0.0 copy-start.5
  1.3 0.0 copy-start.4
  1.3 0.0 copy-start.3
  1.3 0.0 copy-done.5
  1.3 0.7 copy-done.4
  2.0 0.0 copy-done.3
  2.0 0.0 copy-start
  2.0 1.2 %copy-done = bf16[2048,256]{1,0:T(8,128)(2,1)S(1)} copy-done((bf16[2048,256]{1,0:T(8,128)(2,1)S(1)}, bf16[2048,256]{1,0:T(8,128)(2,1)}, u32[]{:S(2)}) %copy-start) | copy-done | bytes 1048600
  3.2 0.0 copy-start.1
  3.2 1.0 %copy-done.1 = f32[512,256]{1,0:T(8,128)S(1)} copy-done((f32[512,256]{1,0:T(8,128)S(1)}, f32[512,256]{1,0:T(8,128)}, u32[]{:S(2)}) %copy-start.1) | copy-done | bytes 524312
  4.3 0.0 copy-start.2
  4.3 0.9 %copy-done.2 = bf16[1,512,256]{2,1,0:T(8,128)(2,1)S(1)} copy-done((bf16[1,512,256]{2,1,0:T(8,128)(2,1)S(1)}, bf16[1,512,256]{2,1,0:T(8,128)(2,1)}, u32[]{:S(2)}) %copy-start.2) | copy-done | bytes 262168
  5.2 0.0 copy-start.6
  5.2 0.7 copy-done.6
  5.9 68.5 %bucket_round.1 = (bf16[2,4,256,256]{3,2,1,0:T(8,128)(2,1)S(1)}, bf16[512,256]{1,0:T(8,128)(2,1)S(1)}, f32[4,8,16,256]{3,2,1,0:T(8,128)S(1)}) custom-call(s32[1,1]{1,0:T(1,128)S(6)} %copy.14.count_ref, bf16[2048,256]{1,0:T(8,128)(2,1)S(1)} %copy-done, bf16[512,256]{1,0:T(8,128)(2,1)S(1)} %bitcast.13, f32[4,8,16,256]{3,2,1,0:T(8,128)S(1)} %bitcast.11, ...), custom_call_target="tpu_custom_call" | custom-call | tf_op jit(solution)/shard_map/bucket_round/pallas_call | solution.py:260
  74.4 1.0 %copy.15 = bf16[2048,256]{1,0:T(8,128)(2,1)} copy(bf16[2048,256]{1,0:T(8,128)(2,1)S(1)} %bitcast.9) | data formatting | bytes 2097152
  75.4 0.7 copy.16
  76.1 0.8 %copy.17 = f32[512,256]{1,0:T(8,128)} copy(f32[512,256]{1,0:T(8,128)S(1)} %bitcast.10) | data formatting | bytes 1048576
Async XLA Ops:
  0.6 0.7 copy-start.5
  1.3 0.7 copy-start.4
  1.3 0.7 copy-start.3
  2.0 1.2 %copy-start = (bf16[2048,256]{1,0:T(8,128)(2,1)S(1)}, bf16[2048,256]{1,0:T(8,128)(2,1)}, u32[]{:S(2)}) copy-start(bf16[2048,256]{1,0:T(8,128)(2,1)} %left_any.1) | copy-start | bytes 3145732
  3.2 1.0 %copy-start.1 = (f32[512,256]{1,0:T(8,128)S(1)}, f32[512,256]{1,0:T(8,128)}, u32[]{:S(2)}) copy-start(f32[512,256]{1,0:T(8,128)} %param.10) | copy-start | bytes 1572868
  4.3 0.9 %copy-start.2 = (bf16[1,512,256]{2,1,0:T(8,128)(2,1)S(1)}, bf16[1,512,256]{2,1,0:T(8,128)(2,1)}, u32[]{:S(2)}) copy-start(bf16[1,512,256]{2,1,0:T(8,128)(2,1)} %param.9) | copy-start | bytes 786436
  5.2 0.7 copy-start.6

commit v3 on v2

--- a/solution.py
+++ b/solution.py
@@ -9,6 +9,7 @@
 
 step_size = 0.5
 relation_step = 12.0
+PARTS = 2
 
 f32, bf16 = jnp.float32, jnp.bfloat16
 VMEM = pltpu.VMEM
@@ -48,7 +49,7 @@
 
 
 def round_kernel(
-    nl, nr,
+    nl, nr, parts,
     count_ref, left_any, right_any, rel_any, src_any, kind_any, dst_any, neg_any,
     left_out, block_out, rel_out,
     left_ref, right_ref, rel_ref, src_ref, kind_ref, dst_ref, neg_ref,
@@ -67,6 +68,7 @@
     negs = neg_ref.shape[1]
     half = width // 2
     piece = ent_l // nr
+    sub = piece // parts
     block = min(256, edges)
     l, r = lax.axis_index("left"), lax.axis_index("right")
     line, side = r // 2, lax.rem(r, 2)
@@ -160,17 +162,30 @@
     def arrived(dst, sem, axis="right"):
         across(dst, dst, sem, sem, axis, mate if axis == "right" else lefts[0]).wait_recv()
 
+    order = list(range(m - 1, -1, -1))
+    later = sorted(range(1, m), key=lambda k: (-low_bit(k), k))
+    spots = [flip(line, k) for k in range(m)]
+
+    def left_rows(which, c, k):
+        return summed(src_ref, (which * m + spots[k]) * piece + c * sub, sub, heads)
+
+    def to_the_mate(c):
+        for k in order:
+            to_mate[c, k] = left_rows(1 - side, c, k)
+            start(to_mate.at[c, k], pair_in.at[c, k], pair_recv.at[c, k], "right", mate)
+
+    to_the_mate(0)
+
     for peer in lefts:
         rgrad[peer] = summed(kind_ref, peer * (nr * share), nr * share, kinds).reshape(
             nr, share, width
         )
         start(rgrad.at[peer], rel_in.at[l], ra_recv.at[l], "left", peer)
 
-    order = list(range(m - 1, -1, -1))
-    spots = [flip(line, k) for k in range(m)]
+    for c in range(1, parts):
+        to_the_mate(c)
     for k in order:
-        to_mate[k] = summed(src_ref, ((1 - side) * m + spots[k]) * piece, piece, heads)
-        start(to_mate.at[k], pair_in.at[k], pair_recv.at[k], "right", mate)
+        held[0, k] = left_rows(side, 0, k)
 
     total = summed(kind_ref, l * (nr * share), nr * share, kinds).reshape(nr, share, width)
     for peer in lefts:
@@ -180,65 +195,79 @@
     for peer in rights:
         start(rel_part.at[peer], rel_mid.at[r], rb_recv.at[r], "right", peer)
 
-    for k in order:
-        held[k] = summed(src_ref, (side * m + spots[k]) * piece, piece, heads)
+    for c in range(1, parts):
+        for k in order:
+            held[c, k] = left_rows(side, c, k)
 
     grad = matmul(weights[...], low_ref[...], ((0,), (0,))) * times
     hot = one_hot(dst_ref[...], (ent_r, edges), 0)
     grad = grad + joined(matmul(hot, tails[...]))
     block_ref[...] = (right_ref[...].astype(f32) - step_size * grad).astype(bf16)
-    start(block_ref, block_out, block_recv.at[0], "right", lax.rem(r + 1, nr))
-
-    for k in order:
-        arrived(pair_in.at[k], pair_recv.at[k])
-        total = held[k] + pair_in[k]
-        top = low_bit(k) if k else levels
-        for level in range(top):
-            arrived(level_in.at[level, k], level_recv.at[level, k])
-            total = total + level_in[level, k]
-        if k:
-            held[k] = total
-            there = k - (1 << top)
-            start(
-                held.at[k], level_in.at[top, there], level_recv.at[top, there],
-                "right", spots[1 << top] * 2 + side,
-            )
-    own_rows = pl.ds(pl.multiple_of((side * m + line) * piece, piece), piece)
-    left_out[side, line] = (
-        left_ref[own_rows, :].astype(f32) - step_size * total
-    ).astype(bf16)
-
-    def pass_on(k):
-        rows = left_out.at[side, spots[k]]
+
+    def rows_of(which, c, k):
+        return left_out.at[which, spots[k], pl.ds(c * sub, sub)]
+
+    def pass_on(c, k):
+        rows = rows_of(side, c, k)
         for level in range((low_bit(k) if k else levels) - 1, -1, -1):
             there = k + (1 << level)
-            start(rows, rows, rows_recv.at[there], "right", spots[1 << level] * 2 + side)
-        start(rows, rows, back_recv.at[k], "right", mate)
-
-    pass_on(0)
-
-    total = rel_part[r]
-    for peer in rights:
-        arrived(rel_mid.at[peer], rb_recv.at[peer])
-        total = total + rel_mid[peer]
-    rel_out[l, r] = rel_ref[l, r] - relation_step * total
-    for peer in rights:
-        start(rel_out.at[l, r], rel_out.at[l, r], rc_recv.at[r], "right", peer)
-
-    later = sorted(range(1, m), key=lambda k: (-low_bit(k), k))
-    for k in later[:1]:
-        arrived(left_out.at[side, spots[k]], rows_recv.at[k])
-        pass_on(k)
+            start(
+                rows, rows, rows_recv.at[c, there], "right",
+                spots[1 << level] * 2 + side,
+            )
+        start(rows, rows, back_recv.at[c, k], "right", mate)
+
+    def forward(c, k):
+        arrived(rows_of(side, c, k), rows_recv.at[c, k])
+        pass_on(c, k)
+
+    for c in range(parts):
+        waiting = list(later) if c else []
+        for k in order:
+            arrived(pair_in.at[c, k], pair_recv.at[c, k])
+            if c == parts - 1 and k == 0:
+                start(block_ref, block_out, block_recv.at[0], "right", lax.rem(r + 1, nr))
+            total = held[c, k] + pair_in[c, k]
+            top = low_bit(k) if k else levels
+            for level in range(top):
+                arrived(level_in.at[c, level, k], level_recv.at[c, level, k])
+                total = total + level_in[c, level, k]
+            if k:
+                held[c, k] = total
+                there = k - (1 << top)
+                start(
+                    held.at[c, k], level_in.at[c, top, there],
+                    level_recv.at[c, top, there], "right", spots[1 << top] * 2 + side,
+                )
+            if waiting and k < m - 1 and k:
+                forward(c - 1, waiting.pop(0))
+        first = pl.multiple_of((side * m + line) * piece + c * sub, sub)
+        left_out[side, line, pl.ds(c * sub, sub)] = (
+            left_ref[pl.ds(first, sub), :].astype(f32) - step_size * total
+        ).astype(bf16)
+        pass_on(c, 0)
+        for k in waiting:
+            forward(c - 1, k)
+
+        if c == 0:
+            total = rel_part[r]
+            for peer in rights:
+                arrived(rel_mid.at[peer], rb_recv.at[peer])
+                total = total + rel_mid[peer]
+            rel_out[l, r] = rel_ref[l, r] - relation_step * total
+            for peer in rights:
+                start(rel_out.at[l, r], rel_out.at[l, r], rc_recv.at[r], "right", peer)
+
     for peer in rights:
         arrived(rel_out.at[l, peer], rc_recv.at[peer])
     for peer in lefts:
         start(rel_out.at[l], rel_out.at[l], rd_recv.at[l], "left", peer)
-    for k in later[1:]:
-        arrived(left_out.at[side, spots[k]], rows_recv.at[k])
-        pass_on(k)
-
-    for k in [0] + later:
-        arrived(left_out.at[1 - side, spots[k]], back_recv.at[k])
+    for k in later:
+        forward(parts - 1, k)
+
+    for c in range(parts):
+        for k in [0] + later:
+            arrived(rows_of(1 - side, c, k), back_recv.at[c, k])
     for peer in lefts:
         arrived(rel_out.at[peer], rd_recv.at[peer], "left")
     arrived(block_out, block_recv.at[0])
@@ -253,12 +282,14 @@
     ent_l, width = left.shape
     ent_r, rels = right.shape[0], relations.shape[0]
     piece, share = ent_l // nr, rels // (nl * nr)
+    parts = PARTS if piece % (16 * PARTS) == 0 else 1
+    sub = piece // parts
     whole = pl.BlockSpec(memory_space=VMEM)
     outside = pl.BlockSpec(memory_space=pl.ANY)
     dma = pltpu.SemaphoreType.DMA
-    sends = 2 * (nl - 1) + 2 * (nr - 1) + 1 + m + (m - 1) + (m - 1) + m
+    sends = 2 * (nl - 1) + 2 * (nr - 1) + 1 + parts * (4 * m - 2)
     left_next, moved, relations_next = pl.pallas_call(
-        functools.partial(round_kernel, nl, nr),
+        functools.partial(round_kernel, nl, nr, parts),
         out_shape=(
             jax.ShapeDtypeStruct((2, m, piece, width), bf16),
             jax.ShapeDtypeStruct((ent_r, width), bf16),
@@ -284,16 +315,16 @@
             VMEM((edges, width), bf16),
             VMEM((edges, ent_r), bf16),
             VMEM((ent_r, width), bf16),
-            VMEM((m, piece, width), f32),
-            VMEM((m, piece, width), f32),
-            VMEM((m, piece, width), f32),
-            VMEM((levels, m, piece, width), f32),
+            VMEM((parts, m, sub, width), f32),
+            VMEM((parts, m, sub, width), f32),
+            VMEM((parts, m, sub, width), f32),
+            VMEM((parts, levels, m, sub, width), f32),
             VMEM((nl, nr, share, width), f32),
             VMEM((nl, nr, share, width), f32),
             VMEM((nr, share, width), f32),
             VMEM((nr, share, width), f32),
-            dma((7,)), dma((sends,)), dma((1,)), dma((m,)), dma((levels, m)),
-            dma((m,)), dma((m,)), dma((nl,)), dma((nr,)), dma((nr,)), dma((nl,)),
+            dma((7,)), dma((sends,)), dma((1,)), dma((parts, m)), dma((parts, levels, m)),
+            dma((parts, m)), dma((parts, m)), dma((nl,)), dma((nr,)), dma((nr,)), dma((nl,)),
         ],
         compiler_params=pltpu.CompilerParams(
             collective_id=0, has_side_effects=True, vmem_limit_bytes=44 * 2**20

time: 77.2 us -> 75.5 us (0.978)
  Pallas kernels: 68.5 us -> 66.8 us
    pallas_call x1, Pallas kernels: 68.5 us -> 66.8 us  [bucket_round(): pl.pallas_call(functools.partial(round_kernel, nl, nr, parts), out_shape=...]
where the time goes in v3:
time: 75.5 us; the launch traced here: 75.2 us
  Pallas kernels  66.8 us (88%)
  local copies, waits for them, and re-layouts  7.05 us (9%)
  between operations  1.34 us (2%)
    pallas_call x1, Pallas kernels, bucket_round(): pl.pallas_call(functools.partial(round_kernel, nl, nr, parts), out_shape=...  66.8 us
    unnamed x17, local copies, waits for them, and re-layouts  7.05 us

profile of v3, /device:TPU:0, one launch (start us, length us, event | category | flops | bytes accessed | tf_op | source)
XLA Modules:
  0.0 75.2 jit_solution(5042473510610387949)
XLA Ops:
  0.6 0.0 copy-start.5
  1.3 0.0 copy-start.4
  1.3 0.0 copy-start.3
  1.3 0.0 copy-done.5
  1.3 0.7 copy-done.4
  2.0 0.0 copy-done.3
  2.0 0.0 copy-start
  2.0 1.2 %copy-done = bf16[2048,256]{1,0:T(8,128)(2,1)S(1)} copy-done((bf16[2048,256]{1,0:T(8,128)(2,1)S(1)}, bf16[2048,256]{1,0:T(8,128)(2,1)}, u32[]{:S(2)}) %copy-start) | copy-done | bytes 1048600
  3.2 0.0 copy-start.1
  3.2 1.0 %copy-done.1 = f32[512,256]{1,0:T(8,128)S(1)} copy-done((f32[512,256]{1,0:T(8,128)S(1)}, f32[512,256]{1,0:T(8,128)}, u32[]{:S(2)}) %copy-start.1) | copy-done | bytes 524312
  4.3 0.0 copy-start.2
  4.3 0.9 %copy-done.2 = bf16[1,512,256]{2,1,0:T(8,128)(2,1)S(1)} copy-done((bf16[1,512,256]{2,1,0:T(8,128)(2,1)S(1)}, bf16[1,512,256]{2,1,0:T(8,128)(2,1)}, u32[]{:S(2)}) %copy-start.2) | copy-done | bytes 262168
  5.2 0.0 copy-start.6
  5.2 0.7 copy-done.6
  5.9 66.8 %bucket_round.1 = (bf16[2,4,256,256]{3,2,1,0:T(8,128)(2,1)S(1)}, bf16[512,256]{1,0:T(8,128)(2,1)S(1)}, f32[4,8,16,256]{3,2,1,0:T(8,128)S(1)}) custom-call(s32[1,1]{1,0:T(1,128)S(6)} %copy.14.count_ref, bf16[2048,256]{1,0:T(8,128)(2,1)S(1)} %copy-done, bf16[512,256]{1,0:T(8,128)(2,1)S(1)} %bitcast.13, f32[4,8,16,256]{3,2,1,0:T(8,128)S(1)} %bitcast.11, ...), custom_call_target="tpu_custom_call" | custom-call | tf_op jit(solution)/shard_map/bucket_round/pallas_call | solution.py:291
  72.7 1.0 %copy.15 = bf16[2048,256]{1,0:T(8,128)(2,1)} copy(bf16[2048,256]{1,0:T(8,128)(2,1)S(1)} %bitcast.9) | data formatting | bytes 2097152
  73.7 0.7 copy.16
  74.4 0.8 %copy.17 = f32[512,256]{1,0:T(8,128)} copy(f32[512,256]{1,0:T(8,128)S(1)} %bitcast.10) | data formatting | bytes 1048576
Async XLA Ops:
  0.6 0.7 copy-start.5
  1.3 0.7 copy-start.4
  1.3 0.7 copy-start.3
  2.0 1.2 %copy-start = (bf16[2048,256]{1,0:T(8,128)(2,1)S(1)}, bf16[2048,256]{1,0:T(8,128)(2,1)}, u32[]{:S(2)}) copy-start(bf16[2048,256]{1,0:T(8,128)(2,1)} %left_any.1) | copy-start | bytes 3145732
  3.2 1.0 %copy-start.1 = (f32[512,256]{1,0:T(8,128)S(1)}, f32[512,256]{1,0:T(8,128)}, u32[]{:S(2)}) copy-start(f32[512,256]{1,0:T(8,128)} %param.10) | copy-start | bytes 1572868
  4.3 0.9 %copy-start.2 = (bf16[1,512,256]{2,1,0:T(8,128)(2,1)S(1)}, bf16[1,512,256]{2,1,0:T(8,128)(2,1)}, u32[]{:S(2)}) copy-start(bf16[1,512,256]{2,1,0:T(8,128)(2,1)} %param.9) | copy-start | bytes 786436
  5.2 0.7 copy-start.6
